TPU v7x, 32 devices: a whole 2x2x4 slice. The times are simulated.
32 devices in a mesh: dp: 4 (over y, x), expert: 8 (over z, core).
Axes of the slice: x: 2, y: 2, z: 4, core: 2. Of those that a mesh axis runs over, the one named last changes fastest.
Arguments:
- tokens: bfloat16 [4096, 1024], P(('dp', 'expert')), may hold values from -6 to 6
- expert_id: int32 [4096, 1], P(('dp', 'expert')), may hold values from 0 to 7; in each aligned block of 128 rows (0 to 127, 128 to 255, ...) at most 32 rows name the same one
- gate_prob: bfloat16 [4096], P(('dp', 'expert')), may hold values from 0.29882812 to 1
- w_in: bfloat16 [8, 1024, 4096], P('expert', None, 'dp'), may hold values from -0.1875 to 0.1875
- w_out: bfloat16 [8, 4096, 1024], P('expert', 'dp'), may hold values from -0.09375 to 0.09375
- head: bfloat16 [1024, 512], replicated, may hold values from -0.1875 to 0.1875
- image_cache: bfloat16 [256, 512], P(('dp', 'expert')), may hold values from -25 to 25
- text_cache: bfloat16 [256, 512], P(('dp', 'expert')), may hold values from -5.1 to 5.1
- pair_label: int32 [256], P(('dp', 'expert')), may hold values from 0 to 255, each once
Outputs:
- grad_image: float32 [256, 512], P(('dp', 'expert'))
- grad_in: float32 [8, 1024, 4096], P('expert', None, 'dp')
- grad_out: float32 [8, 4096, 1024], P('expert', 'dp')
Inputs may be any that keep to these rules, and one draw needn't show every extreme that they name: `expert_id`: among the 128 tokens of one device no expert is named more than 32 times, a bound that some block reaches. `pair_label`: each caption index appears once.
All inputs are finite; a program needn't handle non-finite values.
Results may differ from a plain program's by a relative error of at most 0.015.
Values may be sent and summed in bfloat16 or wider, within the bound.
A program may use at most 64 MiB of HBM per device.

v0:
```python
import jax
import jax.numpy as jnp
from jax import lax
from jax.sharding import PartitionSpec as P

LOGIT_SCALE = 0.125
GELU_K = 0.7978845608
GELU_C = 0.044715


def gelu_parts(pre):
    inner = GELU_K * (pre + GELU_C * pre * pre * pre)
    tangent = jnp.tanh(inner)
    value = 0.5 * pre * (1.0 + tangent)
    slope = 0.5 * (1.0 + tangent) + 0.5 * pre * (1.0 - tangent * tangent) * GELU_K * (
        1.0 + 3.0 * GELU_C * pre * pre
    )
    return (value, slope)


def expert_terms(x_rows, dy_rows, first, second):
    pre = jnp.dot(x_rows, first, preferred_element_type=jnp.float32)
    value, slope = gelu_parts(pre)
    hidden = value.astype(jnp.bfloat16)
    back = lax.dot_general(
        dy_rows, second, (((1,), (1,)), ((), ())), preferred_element_type=jnp.float32
    )
    hidden_grad = (back * slope).astype(jnp.bfloat16)
    grad_first = lax.dot_general(
        x_rows, hidden_grad, (((0,), (0,)), ((), ())), preferred_element_type=jnp.float32
    )
    grad_second = lax.dot_general(
        hidden, dy_rows, (((0,), (0,)), ((), ())), preferred_element_type=jnp.float32
    )
    return (grad_first, grad_second)


def caption_block(carry, image_cache, pair_label, piece):
    run_top, run_total, run_mix, run_label = carry
    logits = LOGIT_SCALE * lax.dot_general(
        image_cache, piece, (((1,), (1,)), ((), ())), preferred_element_type=jnp.float32
    )
    new_top = jnp.maximum(run_top, jnp.max(logits, axis=1, keepdims=True))
    expo = jnp.exp(logits - new_top)
    new_total = jnp.sum(expo, axis=1, keepdims=True)
    new_mix = jnp.dot(expo.astype(jnp.bfloat16), piece, preferred_element_type=jnp.float32)
    columns = jnp.arange(piece.shape[0], dtype=jnp.int32)
    hits = (pair_label[:, None] == columns[None, :]).astype(jnp.bfloat16)
    new_label = jnp.dot(hits, piece, preferred_element_type=jnp.float32)
    return (new_top, new_total, new_mix, new_label)


def body(tokens, expert_id, gate_prob, w_in, w_out, head, image_cache, text_cache, pair_label):
    n_tok = tokens.shape[0]
    n_exp = lax.axis_size("expert")
    capacity = 2 * n_tok // n_exp
    n_pairs = image_cache.shape[0]
    width = image_cache.shape[1]
    start_carry = (
        jnp.full((n_pairs, 1), -1e30, jnp.float32),
        jnp.zeros((n_pairs, 1), jnp.float32),
        jnp.zeros((n_pairs, width), jnp.float32),
        jnp.zeros((n_pairs, width), jnp.float32),
    )
    captions = lax.all_gather(text_cache, ("dp", "expert"), axis=0, tiled=True)
    result = caption_block(start_carry, image_cache, pair_label, captions)
    grad_image = LOGIT_SCALE * (result[2] / result[1] - result[3])
    rep_grad = grad_image[0].astype(jnp.bfloat16)
    cotangent = jnp.dot(head, rep_grad, preferred_element_type=jnp.float32).astype(jnp.bfloat16)
    chosen = expert_id[:, 0]
    onehot = (chosen[:, None] == jnp.arange(n_exp, dtype=jnp.int32)[None, :]).astype(jnp.float32)
    lower = (jnp.arange(n_tok)[:, None] > jnp.arange(n_tok)[None, :]).astype(jnp.float32)
    before = jnp.dot(lower, onehot, precision=lax.Precision.HIGHEST)
    rank = jnp.sum(before * onehot, axis=1).astype(jnp.int32)
    position = chosen * capacity + rank
    dispatch = (position[:, None] == jnp.arange(n_exp * capacity, dtype=jnp.int32)[None, :]).astype(
        jnp.bfloat16
    )
    x_buffer = lax.dot_general(
        dispatch, tokens, (((0,), (0,)), ((), ())), preferred_element_type=jnp.float32
    ).astype(jnp.bfloat16)
    first = w_in[0]
    second = w_out[0]
    out_grad = (
        gate_prob.astype(jnp.float32)[:, None] * cotangent.astype(jnp.float32)[None, :]
    ).astype(jnp.bfloat16)
    g_buffer = lax.dot_general(
        dispatch, out_grad, (((0,), (0,)), ((), ())), preferred_element_type=jnp.float32
    ).astype(jnp.bfloat16)
    x_recv, g_recv = (
        lax.all_to_all(x_buffer, "expert", split_axis=0, concat_axis=0, tiled=True),
        lax.all_to_all(g_buffer, "expert", split_axis=0, concat_axis=0, tiled=True),
    )
    grads = expert_terms(
        lax.all_gather(x_recv, "dp", axis=0, tiled=True),
        lax.all_gather(g_recv, "dp", axis=0, tiled=True),
        first,
        second,
    )
    return (grad_image, grads[0][None], grads[1][None])


def solution(mesh):
    placed = (
        P(("dp", "expert"), None),
        P(("dp", "expert"), None),
        P(("dp", "expert")),
        P("expert", None, "dp"),
        P("expert", "dp", None),
        P(),
        P(("dp", "expert"), None),
        P(("dp", "expert"), None),
        P(("dp", "expert")),
    )
    return jax.shard_map(
        body,
        mesh=mesh,
        in_specs=placed,
        out_specs=(P(("dp", "expert"), None), P("expert", None, "dp"), P("expert", "dp", None)),
        check_vma=False,
    )
```

profile of v0, /device:TPU:0, one launch (start us, length us, event | category | flops | bytes accessed | tf_op | source)
XLA Modules:
  0.0 154.3 jit_solution(10332305750965186248)
XLA Ops:
  7.2 0.0 copy-start
  7.2 0.0 all-gather.3.cloned.1.call-start
  7.2 1.0 fusion.17
  8.2 0.7 fusion.31
  8.9 1.3 convolution_convert_fusion.1
  10.2 21.6 %all_to_all.24 = bf16[8,32,1024]{2,1,0:T(8,128)(2,1)} all-to-all(bf16[8,32,1024]{2,1,0:T(8,128)(2,1)S(1)} %bitcast.40), channel_id=1, replica_groups=mesh['dp'=4,'expert'=8] {'expert'}, dimensions={0} | all-to-all | bytes 1048576 | tf_op jit(solution)/shard_map/all_to_all | solution.py:91
  31.8 0.0 all-gather.3.cloned.1.call-update
  31.8 0.0 all-gather.5.cloned.1.call-start
  31.9 0.7 convert_element_type.52
  32.5 41.0 %all_gather.9 = bf16[256,512]{1,0:T(8,128)(2,1)S(1)} all-gather(bf16[8,512]{1,0:T(8,128)(2,1)} %param.16), channel_id=1, replica_groups=mesh['dp'=4,'expert'=8] {'dp','expert'}, dimensions={0}, use_global_device_ids=true | all-gather | bytes 270336 | tf_op jit(solution)/shard_map/all_gather | solution.py:65
  73.5 1.0 fusion.41
  74.5 0.2 fusion.22
  74.7 0.2 convolution_divide_fusion
  74.9 0.9 fusion.16
  75.8 0.0 copy-start.1
  75.8 1.6 %fusion.28 = f32[1,1024]{1,0:T(1,128)S(1)} fusion(bf16[1024,512]{1,0:T(8,128)(2,1)} %param.14, f32[8,512]{1,0:T(8,128)S(1)} %fusion.16), kind=kOutput, calls=%fused_computation.43 | convolution fusion | flops 1048576 | bytes 1054720 | tf_op jit(solution)/shard_map/dot_general | solution.py:69
  77.4 0.4 convolution_convert_fusion
  77.8 18.5 %all_to_all.25 = bf16[8,32,1024]{2,1,0:T(8,128)(2,1)} all-to-all(bf16[8,32,1024]{2,1,0:T(8,128)(2,1)S(1)} %bitcast.39), channel_id=1, replica_groups=mesh['dp'=4,'expert'=8] {'expert'}, dimensions={0} | all-to-all | bytes 1048576 | tf_op jit(solution)/shard_map/all_to_all | solution.py:92
  96.3 0.0 all-gather.5.cloned.1.call-update
  96.3 0.0 all-gather.3.cloned.1.call-done
  96.3 0.0 copy-done
  96.3 5.9 %fusion.7 = f32[1024,1024]{1,0:T(8,128)} fusion(bf16[1024,1024]{1,0:T(8,128)(2,1)} %all-gather.3.cloned.1.call-done, bf16[1,1024,1024]{2,1,0:T(8,128)(2,1)S(1)} %copy-done), kind=kOutput, calls=%fused_computation.12 | convolution fusion | flops 2147483648 | bytes 8388608 | tf_op jit(solution)/shard_map/dot_general | solution.py:22
  102.2 0.0 copy-done.1
  102.2 26.6 %all-gather.5.cloned.1.call-done = bf16[1024,1024]{1,0:T(8,128)(2,1)} async-done(((bf16[256,1024]{1,0:T(8,128)(2,1)}), bf16[1024,1024]{1,0:T(8,128)(2,1)}) %all-gather.5.cloned.1.call-update) | async-done | bytes 2097168 | tf_op jit(solution)/shard_map/all_gather | solution.py:96
  128.8 7.7 %convolution_bitcast_fusion = f32[1,1024,1024]{2,1,0:T(8,128)} fusion(bf16[1024,1024]{1,0:T(8,128)(2,1)} %all-gather.5.cloned.1.call-done, f32[1024,1024]{1,0:T(8,128)} %fusion.7), kind=kOutput, calls=%fused_computation.10 | convolution fusion | flops 2156920832 | bytes 10485760 | tf_op jit(solution)/shard_map/dot_general | solution.py:32
  136.5 10.9 %convolution_bitcast_fusion.1 = f32[1,1024,1024]{2,1,0:T(8,128)} fusion(bf16[1024,1024]{1,0:T(8,128)(2,1)} %all-gather.3.cloned.1.call-done, f32[1024,1024]{1,0:T(8,128)} %fusion.7, bf16[1024,1024]{1,0:T(8,128)(2,1)} %all-gather.5.cloned.1.call-done, bf16[1,1024,1024]{2,1,0:T(8,128)(2,1)} %param.13), kind=kOutput, calls=%fused_computation.11 | convolution fusion | flops 4314890240 | bytes 14680064 | tf_op jit(solution)/shard_map/dot_general | solution.py:29
  (2 shorter events, 0.0 us)
Async XLA Ops:
  7.2 89.1 %copy-start = (bf16[1,1024,1024]{2,1,0:T(8,128)(2,1)S(1)}, bf16[1,1024,1024]{2,1,0:T(8,128)(2,1)}, u32[]{:S(2)}) copy-start(bf16[1,1024,1024]{2,1,0:T(8,128)(2,1)} %param.12) | copy-start | bytes 6291460
  7.2 89.1 %all-gather.3.cloned.1.call-start = ((), (), s32[]{:S(2)}) async-start(), calls=%async_computation.2 | async-start | bytes 2621440 | tf_op jit(solution)/shard_map/all_gather | solution.py:95
  31.8 97.0 %all-gather.5.cloned.1.call-start = ((), (), s32[]{:S(2)}) async-start(), calls=%async_computation.3 | async-start | bytes 2621440 | tf_op jit(solution)/shard_map/all_gather | solution.py:96
  75.8 26.4 %copy-start.1 = (f32[8,512]{1,0:T(8,128)}, f32[8,512]{1,0:T(8,128)S(1)}, u32[]{:S(2)}) copy-start(f32[8,512]{1,0:T(8,128)S(1)} %fusion.16) | copy-start | bytes 49156
Sparse Core Ops, SparseCore 0:
  32.0 34.8 all-gather.2
  96.4 32.3 all-gather.4
where the time goes:
time: 155 us; the launch traced here: 154 us
  blocking collectives  81 us (52%)
  matrix products  30.8 us (20%)
  waiting for transfers between devices  26.7 us (17%)
  between operations  14.1 us (9%)
    all_gather x1, blocking collectives, body(): captions = lax.all_gather(text_cache, ('dp', 'expert'), axis=0, tiled=True)  41 us
    all_gather x1, waiting for transfers between devices, body(): lax.all_gather(g_recv, 'dp', axis=0, tiled=True)  26.6 us
    all_to_all x1, blocking collectives, body(): lax.all_to_all(x_buffer, 'expert', split_axis=0, concat_axis=0, tiled=True)  21.6 us
    all_to_all x1, blocking collectives, body(): lax.all_to_all(g_buffer, 'expert', split_axis=0, concat_axis=0, tiled=True)  18.5 us
    dot_general x1, matrix products, expert_terms(): lax.dot_general(x_rows, hidden_grad, (((0,), (0,)), ((), ())), preferred_...  10.9 us
    dot_general x1, matrix products, expert_terms(): lax.dot_general(hidden, dy_rows, (((0,), (0,)), ((), ())), preferred_elem...  7.66 us
    dot_general x1, matrix products, expert_terms(): pre = jnp.dot(x_rows, first, preferred_element_type=jnp.float32)  5.86 us
  transfers between devices with their start and end apart: 2, of which 1 were waited for; matrix products, arithmetic and copies ran while one was open for 7% of the time, Pallas kernels for 0%

commit v1 on v0

--- a/solution.py
+++ b/solution.py
@@ -18,19 +18,23 @@
     return (value, slope)
 
 
-def expert_terms(x_rows, dy_rows, first, second):
+def expert_terms(x_rows, gates, cots, first, second, capacity):
+    n_img = cots.shape[0]
     pre = jnp.dot(x_rows, first, preferred_element_type=jnp.float32)
     value, slope = gelu_parts(pre)
-    hidden = value.astype(jnp.bfloat16)
+    hidden = value.astype(jnp.bfloat16).astype(jnp.float32)
     back = lax.dot_general(
-        dy_rows, second, (((1,), (1,)), ((), ())), preferred_element_type=jnp.float32
+        cots, second, (((1,), (1,)), ((), ())), preferred_element_type=jnp.float32
     )
-    hidden_grad = (back * slope).astype(jnp.bfloat16)
+    units = back.shape[1]
+    gated = gates.astype(jnp.float32).reshape(n_img, capacity, 1)
+    hidden_grad = (gated * back[:, None, :] * slope.reshape(n_img, capacity, units)).astype(jnp.bfloat16)
     grad_first = lax.dot_general(
-        x_rows, hidden_grad, (((0,), (0,)), ((), ())), preferred_element_type=jnp.float32
+        x_rows, hidden_grad.reshape(-1, units), (((0,), (0,)), ((), ())), preferred_element_type=jnp.float32
     )
+    summed = jnp.sum(gated * hidden.reshape(n_img, capacity, units), axis=1).astype(jnp.bfloat16)
     grad_second = lax.dot_general(
-        hidden, dy_rows, (((0,), (0,)), ((), ())), preferred_element_type=jnp.float32
+        summed, cots, (((0,), (0,)), ((), ())), preferred_element_type=jnp.float32
     )
     return (grad_first, grad_second)
 
@@ -76,26 +80,18 @@
     dispatch = (position[:, None] == jnp.arange(n_exp * capacity, dtype=jnp.int32)[None, :]).astype(
         jnp.bfloat16
     )
+    width_in = tokens.shape[1]
+    carried = jnp.concatenate(
+        [tokens, jnp.broadcast_to(gate_prob[:, None], (n_tok, 128))], axis=1
+    )
     x_buffer = lax.dot_general(
-        dispatch, tokens, (((0,), (0,)), ((), ())), preferred_element_type=jnp.float32
+        dispatch, carried, (((0,), (0,)), ((), ())), preferred_element_type=jnp.float32
     ).astype(jnp.bfloat16)
-    first = w_in[0]
-    second = w_out[0]
-    out_grad = (
-        gate_prob.astype(jnp.float32)[:, None] * cotangent.astype(jnp.float32)[None, :]
-    ).astype(jnp.bfloat16)
-    g_buffer = lax.dot_general(
-        dispatch, out_grad, (((0,), (0,)), ((), ())), preferred_element_type=jnp.float32
-    ).astype(jnp.bfloat16)
-    x_recv, g_recv = (
-        lax.all_to_all(x_buffer, "expert", split_axis=0, concat_axis=0, tiled=True),
-        lax.all_to_all(g_buffer, "expert", split_axis=0, concat_axis=0, tiled=True),
-    )
+    x_recv = lax.all_to_all(x_buffer, "expert", split_axis=0, concat_axis=0, tiled=True)
+    rows = lax.all_gather(x_recv, "dp", axis=0, tiled=True)
+    cots = lax.all_gather(cotangent[None], ("dp", "expert"), axis=0, tiled=True)
     grads = expert_terms(
-        lax.all_gather(x_recv, "dp", axis=0, tiled=True),
-        lax.all_gather(g_recv, "dp", axis=0, tiled=True),
-        first,
-        second,
+        rows[:, :width_in], rows[:, width_in], cots, w_in[0], w_out[0], capacity
     )
     return (grad_image, grads[0][None], grads[1][None])
 

time: 155 us -> 142 us (0.916)
  waiting for transfers between devices: 26.7 us -> 0.03 us
  blocking collectives: 81 us -> 101 us
  matrix products: 30.8 us -> 21.6 us
  other arithmetic: 1.53 us -> 3.72 us
    all_gather x0 -> x1, blocking collectives: none -> 36.9 us  [body(): cots = lax.all_gather(cotangent[None], ('dp', 'expert'), axis=0, tiled=True)]
    all_gather x2 -> x1, waiting for transfers between devices: 26.7 us -> 0.01 us  [body(): rows = lax.all_gather(x_recv, 'dp', axis=0, tiled=True)]
    all_to_all x1 -> x0, blocking collectives: 18.5 us -> none  [body(): lax.all_to_all(g_buffer, 'expert', split_axis=0, concat_axis=0, tiled=True)]
    dot_general x4, matrix products: 20.4 us -> 10.9 us  [the longest x1 4.46 us: expert_terms(): lax.dot_general(x_rows, hidden_grad.reshape(-1, units), (((0,), (0,)), ((...]
    reduce_sum x0 -> x1, other arithmetic: none -> 1.75 us  [expert_terms(): jnp.sum(gated * hidden.reshape(n_img, capacity, units), axis=1)]
  transfers between devices with their start and end apart: 2 -> 1, of which waited for: 1 -> 0; matrix products, arithmetic and copies ran while one was open for 7% -> 4% of each run, Pallas kernels for 0% -> 0%
where the time goes in v1:
time: 142 us; the launch traced here: 141 us
  blocking collectives  101 us (71%)
  matrix products  21.6 us (15%)
  between operations  14.1 us (10%)
  other arithmetic  3.72 us (3%)
    all_gather x1, blocking collectives, body(): captions = lax.all_gather(text_cache, ('dp', 'expert'), axis=0, tiled=True)  41.1 us
    all_gather x1, blocking collectives, body(): cots = lax.all_gather(cotangent[None], ('dp', 'expert'), axis=0, tiled=True)  36.9 us
    all_to_all x1, blocking collectives, body(): lax.all_to_all(x_buffer, 'expert', split_axis=0, concat_axis=0, tiled=True)  23 us
    dot_general x1, matrix products, expert_terms(): pre = jnp.dot(x_rows, first, preferred_element_type=jnp.float32)  6.13 us
    dot_general x1, matrix products, expert_terms(): lax.dot_general(x_rows, hidden_grad.reshape(-1, units), (((0,), (0,)), ((...  4.46 us
  transfers between devices with their start and end apart: 1, of which 0 were waited for; matrix products, arithmetic and copies ran while one was open for 4% of the time, Pallas kernels for 0%

profile of v1, /device:TPU:0, one launch (start us, length us, event | category | flops | bytes accessed | tf_op | source)
XLA Modules:
  0.0 141.4 jit_solution(8349800901283890605)
XLA Ops:
  7.2 0.0 copy-start
  7.2 0.0 all-gather.3.cloned.1.call-start
  7.2 1.0 fusion.15
  8.2 0.7 fusion.30
  8.9 0.7 broadcast_in_dim.8
  9.6 1.4 convolution_convert_fusion
  11.0 23.0 %all_to_all.12 = bf16[8,32,1152]{2,1,0:T(8,128)(2,1)} all-to-all(bf16[8,32,1152]{2,1,0:T(8,128)(2,1)S(1)} %bitcast.42), channel_id=1, replica_groups=mesh['dp'=4,'expert'=8] {'expert'}, dimensions={0} | all-to-all | bytes 1179648 | tf_op jit(solution)/shard_map/all_to_all | solution.py:90
  34.0 0.0 all-gather.3.cloned.1.call-update
  34.0 41.1 %all_gather.9 = bf16[256,512]{1,0:T(8,128)(2,1)S(1)} all-gather(bf16[8,512]{1,0:T(8,128)(2,1)} %param.16), channel_id=1, replica_groups=mesh['dp'=4,'expert'=8] {'dp','expert'}, dimensions={0}, use_global_device_ids=true | all-gather | bytes 270336 | tf_op jit(solution)/shard_map/all_gather | solution.py:69
  75.2 1.0 fusion.32
  76.1 0.2 fusion.21
  76.3 0.2 convolution_divide_fusion
  76.5 0.9 fusion.14
  77.4 0.0 copy-start.2
  77.4 1.6 %fusion.27 = f32[1,1024]{1,0:T(1,128)S(1)} fusion(bf16[1024,512]{1,0:T(8,128)(2,1)} %param.14, f32[8,512]{1,0:T(8,128)S(1)} %fusion.14), kind=kOutput, calls=%fused_computation.45 | convolution fusion | flops 1048576 | bytes 1054720 | tf_op jit(solution)/shard_map/dot_general | solution.py:73
  79.0 36.9 %all-gather = bf16[32768]{0:T(1024)(128)(2,1)S(1)} all-gather(bf16[1024]{0:T(1024)(128)(2,1)S(1)} %convert_element_type.64), channel_id=2, replica_groups=mesh['dp'=4,'expert'=8] {'dp','expert'}, dimensions={0}, use_global_device_ids=true | all-gather | bytes 67584 | tf_op jit(solution)/shard_map/all_gather | solution.py:92
  115.9 2.3 %fusion.10 = f32[32,1024]{1,0:T(8,128)S(1)} fusion(bf16[32,1024]{1,0:T(8,128)(2,1)S(1)} %reshape.53, bf16[1,1024,1024]{2,1,0:T(8,128)(2,1)} %param.13), kind=kOutput, calls=%fused_computation.18 | convolution fusion | flops 67108864 | bytes 2293760 | tf_op jit(solution)/shard_map/dot_general | solution.py:26
  118.2 0.0 all-gather.3.cloned.1.call-done
  118.2 1.1 convert_reduce_fusion
  119.3 0.1 reshape.50
  119.4 0.0 copy-done
  119.4 6.1 %fusion.6 = (bf16[1024,1024]{1,0:T(8,128)(2,1)S(1)}, f32[1024,1024]{1,0:T(8,128)S(1)}) fusion(f32[32,1024]{1,0:T(8,128)S(1)} %fusion.10, f32[1024]{0:T(1024)S(1)} %convert_reduce_fusion, bf16[1,1024,1024]{2,1,0:T(8,128)(2,1)S(1)} %copy-done, bf16[1024,1152]{1,0:T(8,128)(2,1)} %all-gather.3.cloned.1.call-done), kind=kOutput, calls=%fused_computation.8 | convolution fusion | flops 2168455168 | bytes 10620928 | tf_op jit(solution)/shard_map/dot_general | solution.py:23
  125.6 0.0 copy-done.2
  125.6 0.0 copy-start.1
  125.6 1.8 %fusion.7 = bf16[32,1024]{1,0:T(8,128)(2,1)S(1)} fusion(f32[32,32]{1,0:T(8,128)S(1)} %reshape.50, f32[1024,1024]{1,0:T(8,128)S(1)} %get-tuple-element.6), kind=kLoop, calls=%fused_computation.10 | loop fusion | flops 12550144 | bytes 4263936 | tf_op jit(solution)/shard_map/reduce_sum | solution.py:35
  127.3 2.7 %convolution_bitcast_fusion = f32[1,1024,1024]{2,1,0:T(8,128)} fusion(bf16[32,1024]{1,0:T(8,128)(2,1)S(1)} %reshape.53, bf16[32,1024]{1,0:T(8,128)(2,1)S(1)} %fusion.7), kind=kOutput, calls=%fused_computation.14 | convolution fusion | flops 67108864 | bytes 4325376 | tf_op jit(solution)/shard_map/dot_general | solution.py:36
  130.1 0.0 copy-done.1
  130.1 4.5 %convolution_bitcast_fusion.1 = f32[1,1024,1024]{2,1,0:T(8,128)} fusion(bf16[1024,1024]{1,0:T(8,128)(2,1)S(1)} %get-tuple-element.5, bf16[1024,1152]{1,0:T(8,128)(2,1)S(1)} %copy-done.1), kind=kOutput, calls=%fused_computation.15 | convolution fusion | flops 2147483648 | bytes 8388608 | tf_op jit(solution)/shard_map/dot_general | solution.py:32
  (3 shorter events, 0.0 us)
Async XLA Ops:
  7.2 112.3 %copy-start = (bf16[1,1024,1024]{2,1,0:T(8,128)(2,1)S(1)}, bf16[1,1024,1024]{2,1,0:T(8,128)(2,1)}, u32[]{:S(2)}) copy-start(bf16[1,1024,1024]{2,1,0:T(8,128)(2,1)} %param.12) | copy-start | bytes 6291460
  7.2 111.1 %all-gather.3.cloned.1.call-start = ((), (), s32[]{:S(2)}) async-start(), calls=%async_computation.1 | async-start | bytes 2949120 | tf_op jit(solution)/shard_map/all_gather | solution.py:91
  77.4 48.2 %copy-start.2 = (f32[8,512]{1,0:T(8,128)}, f32[8,512]{1,0:T(8,128)S(1)}, u32[]{:S(2)}) copy-start(f32[8,512]{1,0:T(8,128)S(1)} %fusion.14) | copy-start | bytes 49156
  125.6 4.5 %copy-start.1 = (bf16[1024,1152]{1,0:T(8,128)(2,1)S(1)}, bf16[1024,1152]{1,0:T(8,128)(2,1)}, u32[]{:S(2)}) copy-start(bf16[1024,1152]{1,0:T(8,128)(2,1)} %all-gather.3.cloned.1.call-done) | copy-start | bytes 7077892
Sparse Core Ops, SparseCore 0:
  34.1 37.1 all-gather.2

commit v2 on v1

v2 whole, which is shorter than its diff:
```python
import functools

import jax
import jax.numpy as jnp
from jax import lax
from jax.experimental import pallas as pl
from jax.experimental.pallas import tpu as pltpu
from jax.sharding import PartitionSpec as P

LOGIT_SCALE = 0.125
GELU_K = 0.7978845608
GELU_C = 0.044715
LANES = 128
BF = jnp.bfloat16
F32 = jnp.float32


def gelu_parts(pre):
    inner = GELU_K * (pre + GELU_C * pre * pre * pre)
    tangent = jnp.tanh(inner)
    value = 0.5 * pre * (1.0 + tangent)
    slope = 0.5 * (1.0 + tangent) + 0.5 * pre * (1.0 - tangent * tangent) * GELU_K * (
        1.0 + 3.0 * GELU_C * pre * pre
    )
    return (value, slope)


def dot_t(a, b):
    return lax.dot_general(a, b, (((1,), (1,)), ((), ())), preferred_element_type=F32)


def kernel(
    n_dp, n_exp, capacity,
    tokens_ref, id_ref, gate_ref, image_ref, text_ref, label_ref, head_hbm, w_in_hbm, w_out_hbm,
    grad_image_ref, x_ref, hg_ref, sum_ref, cots_ref,
    head_ref, w_in_ref, w_out_ref, xbuf, xall, tall, call, back_ref, sums,
    load_sem, x1_send, x1_recv, x2_send, x2_recv, t1_send, t1_recv, t2_send, t2_recv,
    c1_send, c1_recv, c2_send, c2_recv,
):
    dp = lax.axis_index("dp")
    ex = lax.axis_index("expert")
    n_tok, width = tokens_ref.shape
    wide = xbuf.shape[2]
    slots = n_exp * capacity
    units = w_in_ref.shape[1]

    loads = [
        pltpu.make_async_copy(src, dst, load_sem.at[i])
        for i, (src, dst) in enumerate(
            ((head_hbm, head_ref), (w_in_hbm, w_in_ref), (w_out_hbm, w_out_ref))
        )
    ]
    for load in loads:
        load.start()

    def ex_at(k):
        return lax.rem(ex + k, n_exp)

    def ex_from(k):
        return lax.rem(ex + n_exp - k, n_exp)

    def dp_at(k):
        return lax.rem(dp + k, n_dp)

    def dp_from(k):
        return lax.rem(dp + n_dp - k, n_dp)

    def loop(lo, hi, fn):
        def step(k, c):
            fn(k)
            return c

        lax.fori_loop(lo, hi, step, 0)

    def over_ex(src, dst, send, recv, peer):
        return pltpu.make_async_remote_copy(
            src_ref=src, dst_ref=dst, send_sem=send, recv_sem=recv,
            device_id={"expert": peer}, device_id_type=pl.DeviceIdType.MESH,
        )

    def over_dp(src, dst, send, recv, peer):
        return pltpu.make_async_remote_copy(
            src_ref=src, dst_ref=dst, send_sem=send, recv_sem=recv,
            device_id={"dp": peer}, device_id_type=pl.DeviceIdType.MESH,
        )

    def t1(k, who):
        return over_ex(tall.at[dp, who], tall.at[dp, who], t1_send.at[k], t1_recv.at[who], ex_at(k))

    def c1(k, who):
        return over_ex(call.at[dp, who], call.at[dp, who], c1_send.at[k], c1_recv.at[who], ex_at(k))

    def x1(k, block, who):
        return over_ex(xbuf.at[block], xall.at[dp, who], x1_send.at[k], x1_recv.at[who], ex_at(k))

    def t2(k, row):
        return over_dp(tall.at[row], tall.at[row], t2_send.at[k], t2_recv.at[row], dp_at(k))

    def c2(k, row):
        return over_dp(call.at[row], call.at[row], c2_send.at[k], c2_recv.at[row], dp_at(k))

    def x2(k, row, j):
        return over_dp(
            xall.at[row, j], xall.at[row, j], x2_send.at[k, j], x2_recv.at[row, j], dp_at(k)
        )

    barrier = pltpu.get_barrier_semaphore()
    loop(1, n_exp, lambda k: pl.semaphore_signal(
        barrier, inc=1, device_id={"expert": ex_at(k)}, device_id_type=pl.DeviceIdType.MESH))
    loop(1, n_dp, lambda k: pl.semaphore_signal(
        barrier, inc=1, device_id={"dp": dp_at(k)}, device_id_type=pl.DeviceIdType.MESH))

    half = text_ref.shape[1] // 2
    text = text_ref[...].astype(F32)
    tall[dp, ex] = jnp.concatenate([text[:, :half], text[:, half:]], axis=0).astype(BF)

    own = jnp.broadcast_to(id_ref[...].astype(F32), (n_tok, n_tok))
    other = own.T
    earlier = lax.broadcasted_iota(jnp.int32, (n_tok, n_tok), 0) < lax.broadcasted_iota(
        jnp.int32, (n_tok, n_tok), 1
    )
    rank = jnp.sum(jnp.where((own == other) & earlier, 1.0, 0.0), axis=0, keepdims=True)
    position = (other[:1] * capacity + rank).astype(jnp.int32)
    dispatch = jnp.where(
        lax.broadcasted_iota(jnp.int32, (slots, n_tok), 0) == position, 1.0, 0.0
    ).astype(BF)
    gate = jnp.broadcast_to(gate_ref[...].astype(F32), (n_tok, n_tok)).T.astype(BF)
    x_slots = jnp.dot(dispatch, tokens_ref[...], preferred_element_type=F32)
    g_slots = jnp.dot(dispatch, gate, preferred_element_type=F32)
    xbuf[:, :, :width] = x_slots.reshape(n_exp, capacity, width).astype(BF)
    xbuf[:, :, width:] = g_slots.reshape(n_exp, capacity, wide - width).astype(BF)

    pl.semaphore_wait(barrier, n_exp - 1 + n_dp - 1)

    loop(1, n_exp, lambda k: t1(k, ex).start())
    loop(1, n_exp, lambda k: x1(k, ex_at(k), ex).start())
    xall[dp, ex] = xbuf[ex]
    loop(1, n_dp, lambda k: x2(k, dp, ex).start())

    loop(1, n_exp, lambda k: t1(k, ex_from(k)).wait_recv())
    loop(1, n_dp, lambda k: t2(k, dp).start())

    def forward(k):
        j = ex_from(k)
        x1(k, ex, j).wait_recv()
        loop(1, n_dp, lambda m: x2(m, dp, j).start())

    middle = n_exp // 2
    loop(1, middle, forward)

    loop(1, n_dp, lambda k: t2(k, dp_from(k)).wait_recv())
    n_img = n_dp * n_exp
    pairs = text_ref.shape[0]
    every = tall[...].astype(F32).reshape(n_img, 2 * pairs, half)
    captions = jnp.concatenate(
        [every[:, :pairs].reshape(n_img * pairs, half), every[:, pairs:].reshape(n_img * pairs, half)],
        axis=1,
    ).astype(BF)
    logits = LOGIT_SCALE * dot_t(image_ref[...], captions)
    expo = jnp.exp(logits - jnp.max(logits, axis=1, keepdims=True))
    total = jnp.sum(expo, axis=1, keepdims=True)
    mixed = jnp.dot(expo.astype(BF), captions, preferred_element_type=F32) / total
    columns = lax.broadcasted_iota(jnp.int32, logits.shape, 1)
    hits = jnp.where(label_ref[...] == columns, 1.0, 0.0).astype(BF)
    grad_image = LOGIT_SCALE * (mixed - jnp.dot(hits, captions, preferred_element_type=F32))
    grad_image_ref[...] = grad_image
    loads[0].wait()
    cotangent = dot_t(grad_image.astype(BF), head_ref[...]).astype(BF).astype(F32)
    for k in range(width // LANES):
        call[dp, ex, k : k + 1, :] = cotangent[:1, k * LANES : (k + 1) * LANES]
    loop(1, n_exp, lambda k: c1(k, ex).start())

    loop(middle, n_exp, forward)

    loop(1, n_exp, lambda k: c1(k, ex_from(k)).wait_recv())
    loop(1, n_dp, lambda k: c2(k, dp).start())
    loads[1].wait()
    loads[2].wait()
    loop(1, n_dp, lambda k: c2(k, dp_from(k)).wait_recv())
    cots = jnp.concatenate(
        [call[:, :, k, :].reshape(n_img, LANES) for k in range(width // LANES)], axis=1
    ).astype(BF)
    cots_ref[...] = cots
    back = dot_t(cots, w_out_ref[...])
    back_ref[...] = back.reshape(n_dp, n_exp, units)

    tile = min(256, units)

    def expert_rows(row):
        block = xall[row]
        if capacity % 16:
            block = block.astype(F32).reshape(slots, wide).astype(BF)
        else:
            block = block.reshape(slots, wide)
        rows = block[:, :width]
        gates = block[:, width : width + LANES].astype(F32)
        gates = jnp.concatenate([gates] * (tile // LANES), axis=1)
        at = pl.ds(pl.multiple_of(row * slots, slots), slots)
        x_ref[at, :] = rows
        for c in range(units // tile):
            cols = slice(c * tile, (c + 1) * tile)
            pre = jnp.dot(rows, w_in_ref[:, cols], preferred_element_type=F32)
            value, slope = gelu_parts(pre)
            hidden = value.astype(BF).astype(F32) * gates
            slope = (slope * gates).reshape(n_exp, capacity, tile)
            hg = slope * back_ref[row, :, cols][:, None, :]
            hg_ref[at, cols] = hg.reshape(slots, tile).astype(BF)
            sums[row, :, cols] = jnp.sum(hidden.reshape(n_exp, capacity, tile), axis=1)

    def remote_rows(k):
        row = dp_from(k)
        loop(0, n_exp, lambda j: x2(k, row, j).wait_recv())
        expert_rows(row)

    expert_rows(dp)
    loop(1, n_dp, remote_rows)
    sum_ref[...] = sums[...].reshape(n_img, units).astype(BF)

    def finish_ex(k):
        t1(k, ex).wait_send()
        c1(k, ex).wait_send()
        x1(k, ex_at(k), ex).wait_send()

    def finish_dp(k):
        t2(k, dp).wait_send()
        c2(k, dp).wait_send()
        loop(0, n_exp, lambda j: x2(k, dp, j).wait_send())

    loop(1, n_exp, finish_ex)
    loop(1, n_dp, finish_dp)


def body(tokens, expert_id, gate_prob, w_in, w_out, head, image_cache, text_cache, pair_label):
    n_tok, width = tokens.shape
    n_exp = lax.axis_size("expert")
    n_dp = lax.axis_size("dp")
    capacity = 2 * n_tok // n_exp
    slots = n_exp * capacity
    n_img = n_dp * n_exp
    units = w_in.shape[2]
    pairs, emb = text_cache.shape
    wide = width + LANES
    vmem = pl.BlockSpec(memory_space=pltpu.VMEM)
    hbm = pl.BlockSpec(memory_space=pl.ANY)
    dma = pltpu.SemaphoreType.DMA
    grad_image, rows, hidden_grad, summed, cots = pl.pallas_call(
        functools.partial(kernel, n_dp, n_exp, capacity),
        out_shape=(
            jax.ShapeDtypeStruct((pairs, emb), F32),
            jax.ShapeDtypeStruct((n_dp * slots, width), BF),
            jax.ShapeDtypeStruct((n_dp * slots, units), BF),
            jax.ShapeDtypeStruct((n_img, units), BF),
            jax.ShapeDtypeStruct((n_img, width), BF),
        ),
        in_specs=[vmem] * 6 + [hbm] * 3,
        out_specs=(vmem,) * 5,
        scratch_shapes=[
            pltpu.VMEM(head.shape, BF),
            pltpu.VMEM((width, units), BF),
            pltpu.VMEM((units, width), BF),
            pltpu.VMEM((n_exp, capacity, wide), BF),
            pltpu.VMEM((n_dp, n_exp, capacity, wide), BF),
            pltpu.VMEM((n_dp, n_exp, 2 * pairs, emb // 2), BF),
            pltpu.VMEM((n_dp, n_exp, width // LANES, LANES), F32),
            pltpu.VMEM((n_dp, n_exp, units), F32),
            pltpu.VMEM((n_dp, n_exp, units), F32),
            dma((3,)),
            dma((n_exp,)), dma((n_exp,)), dma((n_dp, n_exp)), dma((n_dp, n_exp)),
            dma((n_exp,)), dma((n_exp,)), dma((n_dp,)), dma((n_dp,)),
            dma((n_exp,)), dma((n_exp,)), dma((n_dp,)), dma((n_dp,)),
        ],
        compiler_params=pltpu.CompilerParams(
            collective_id=0, has_side_effects=True, vmem_limit_bytes=56 * 2**20
        ),
    )(
        tokens, expert_id, gate_prob.reshape(1, n_tok), image_cache, text_cache,
        pair_label.reshape(pairs, 1), head, w_in[0], w_out[0],
    )
    grad_first = lax.dot_general(
        rows, hidden_grad, (((0,), (0,)), ((), ())), preferred_element_type=F32
    )
    grad_second = lax.dot_general(
        summed, cots, (((0,), (0,)), ((), ())), preferred_element_type=F32
    )
    return (grad_image, grad_first[None], grad_second[None])


def solution(mesh):
    placed = (
        P(("dp", "expert"), None),
        P(("dp", "expert"), None),
        P(("dp", "expert")),
        P("expert", None, "dp"),
        P("expert", "dp", None),
        P(),
        P(("dp", "expert"), None),
        P(("dp", "expert"), None),
        P(("dp", "expert")),
    )
    return jax.shard_map(
        body,
        mesh=mesh,
        in_specs=placed,
        out_specs=(P(("dp", "expert"), None), P("expert", None, "dp"), P("expert", "dp", None)),
        check_vma=False,
    )
```

time: 142 us -> 68.3 us (0.48)
  blocking collectives: 101 us -> 0 us
  Pallas kernels: 0 us -> 54.7 us
  between operations: 14.1 us -> 0.66 us
  matrix products: 21.6 us -> 9.4 us
  other arithmetic: 3.72 us -> 0 us
  local copies, waits for them, and re-layouts: 0.85 us -> 3.33 us
    all_gather x2 -> x0, blocking collectives: 78 us -> none  [the longest x1 41.1 us: body(): captions = lax.all_gather(text_cache, ('dp', 'expert'), axis=0, tiled=True)]
    pallas_call x0 -> x1, Pallas kernels: none -> 54.7 us  [body(): pl.pallas_call(functools.partial(kernel, n_dp, n_exp, capacity), out_shap...]
    all_to_all x1 -> x0, blocking collectives: 23 us -> none  [body(): lax.all_to_all(x_buffer, 'expert', split_axis=0, concat_axis=0, tiled=True)]
    dot_general x10 -> x2, matrix products: 21.6 us -> 9.4 us  [the longest x1 6.65 us: body(): lax.dot_general(rows, hidden_grad, (((0,), (0,)), ((), ())), preferred_el...]
    unnamed x6 -> x8, local copies, waits for them, and re-layouts: 0.02 us -> 2.01 us
    reduce_sum x2 -> x0, other arithmetic: 1.94 us -> none  [the longest x1 1.75 us: expert_terms(): jnp.sum(gated * hidden.reshape(n_img, capacity, units), axis=1)]
  transfers between devices with their start and end apart: 1 -> 0, of which waited for: 0 -> 0; matrix products, arithmetic and copies ran while one was open for 4% -> 0% of each run, Pallas kernels for 0% -> 0%
where the time goes in v2:
time: 68.3 us; the launch traced here: 68.1 us
  Pallas kernels  54.7 us (80%)
  matrix products  9.4 us (14%)
  local copies, waits for them, and re-layouts  3.33 us (5%)
    pallas_call x1, Pallas kernels, body(): pl.pallas_call(functools.partial(kernel, n_dp, n_exp, capacity), out_shap...  54.7 us
    dot_general x1, matrix products, body(): lax.dot_general(rows, hidden_grad, (((0,), (0,)), ((), ())), preferred_el...  6.65 us
    dot_general x1, matrix products, body(): lax.dot_general(summed, cots, (((0,), (0,)), ((), ())), preferred_element...  2.75 us
    unnamed x8, local copies, waits for them, and re-layouts  2.01 us

profile of v2, /device:TPU:0, one launch (start us, length us, event | category | flops | bytes accessed | tf_op | source)
XLA Modules:
  0.0 68.1 jit_solution(5333934170364394817)
XLA Ops:
  0.6 1.3 %copy.13.label_ref = s32[8,1]{1,0:T(8,128)} copy(s32[8,1]{0,1:T(1,128)} %bitcast.15) | data formatting | bytes 64 | tf_op jit(solution)/shard_map/reshape | solution.py:277
  2.0 1.4 %copy.12.id_ref = s32[128,1]{1,0:T(8,128)} copy(s32[128,1]{0,1:T(1,128)} %param.10) | data formatting | bytes 1024 | tf_op args[1]
  3.3 54.7 %shard_map.112 = (f32[8,512]{1,0:T(8,128)}, bf16[1024,1024]{1,0:T(8,128)(2,1)}, bf16[1024,1024]{1,0:T(8,128)(2,1)}, bf16[32,1024]{1,0:T(8,128)(2,1)}, bf16[32,1024]{1,0:T(8,128)(2,1)}) custom-call(bf16[128,1024]{1,0:T(8,128)(2,1)} %tokens_ref.1, s32[128,1]{1,0:T(8,128)} %copy.12.id_ref, bf16[1,128]{1,0:T(2,128)(2,1)} %bitcast.14, bf16[8,512]{1,0:T(8,128)(2,1)} %image_ref.1, ...), custom_call_target="tpu_custom_call" | custom-call | tf_op jit(solution)/shard_map/pallas_call | solution.py:246
  58.1 0.0 copy-start
  58.1 0.0 copy-start.1
  58.1 6.7 %convolution_bitcast_fusion.1 = f32[1,1024,1024]{2,1,0:T(8,128)} fusion(bf16[1024,1024]{1,0:T(8,128)(2,1)} %get-tuple-element.9, bf16[1024,1024]{1,0:T(8,128)(2,1)} %get-tuple-element.10), kind=kOutput, calls=%fused_computation.1 | convolution fusion | flops 2147483648 | bytes 8388608 | tf_op jit(solution)/shard_map/dot_general | solution.py:279
  64.7 0.0 copy-done
  64.8 0.0 copy-done.1
  64.8 0.0 copy-start.2
  64.8 2.7 %convolution_bitcast_fusion = f32[1,1024,1024]{2,1,0:T(8,128)} fusion(bf16[32,1024]{1,0:T(8,128)(2,1)S(1)} %copy-done, bf16[32,1024]{1,0:T(8,128)(2,1)S(1)} %copy-done.1), kind=kOutput, calls=%fused_computation | convolution fusion | flops 67108864 | bytes 4325376 | tf_op jit(solution)/shard_map/dot_general | solution.py:282
  67.5 0.0 copy-done.2
  67.5 0.6 copy.15
Async XLA Ops:
  58.1 6.7 %copy-start = (bf16[32,1024]{1,0:T(8,128)(2,1)S(1)}, bf16[32,1024]{1,0:T(8,128)(2,1)}, u32[]{:S(2)}) copy-start(bf16[32,1024]{1,0:T(8,128)(2,1)} %get-tuple-element.11) | copy-start | bytes 196612
  58.1 6.7 %copy-start.1 = (bf16[32,1024]{1,0:T(8,128)(2,1)S(1)}, bf16[32,1024]{1,0:T(8,128)(2,1)}, u32[]{:S(2)}) copy-start(bf16[32,1024]{1,0:T(8,128)(2,1)} %get-tuple-element.12) | copy-start | bytes 196612
  64.8 2.8 %copy-start.2 = (f32[8,512]{1,0:T(8,128)S(1)}, f32[8,512]{1,0:T(8,128)}, u32[]{:S(2)}) copy-start(f32[8,512]{1,0:T(8,128)} %get-tuple-element.16) | copy-start | bytes 49156
